TPU v7x, 128 devices: a whole 4x4x4 slice. The times are simulated.
128 devices in a mesh: fsdp: 16 (over y_hi, z, core), tp: 8 (over x, y_lo).
Axes of the slice: x: 4, y: 4 (y_hi: 2, y_lo: 2; y = y_hi * 2 + y_lo), z: 4, core: 2. Of those that a mesh axis runs over, the one named last changes fastest.
Arguments:
- normed: bfloat16 [2, 256, 16384], P(None, None, 'fsdp'), may hold values from -6 to 6
- resident_gate_matrix: bfloat16 [16384, 26624], P('fsdp', 'tp'), may hold values from -0.046875 to 0.046875
- resident_up_matrix: bfloat16 [16384, 26624], P('fsdp', 'tp'), may hold values from -0.046875 to 0.046875
- resident_down_matrix: bfloat16 [26624, 16384], P('tp', 'fsdp'), may hold values from -0.0390625 to 0.0390625
- gate_input_factor: bfloat16 [16, 16384], P(None, ('fsdp', 'tp')), may hold values from -0.046875 to 0.046875
- up_input_factor: bfloat16 [16, 16384], P(None, ('fsdp', 'tp')), may hold values from -0.046875 to 0.046875
- gate_output_factor: bfloat16 [26624, 16], P(('tp', 'fsdp')), may hold values from -0.29882812 to 0.29882812
- up_output_factor: bfloat16 [26624, 16], P(('tp', 'fsdp')), may hold values from -0.29882812 to 0.29882812
- down_input_factor: bfloat16 [16, 26624], P(None, ('tp', 'fsdp')), may hold values from -0.0390625 to 0.0390625
- down_output_factor: bfloat16 [16384, 16], P(('fsdp', 'tp')), may hold values from -0.29882812 to 0.29882812
Outputs:
- mixed: bfloat16 [2, 256, 16384], P(None, 'tp', 'fsdp')
All inputs are finite; a program needn't handle non-finite values.
Results may differ from a plain program's by a relative error of at most 0.007.
Values may be sent and summed in bfloat16 or wider, within the bound.
No kernel may reach another device: no remote copies, remote signals or barrier semaphores. Data moves between devices by JAX's collectives and lax.ppermute only.
A program may use at most 128 MiB of HBM per device.

v0:
```python
import jax
import jax.numpy as jnp
from jax import lax
from jax.sharding import PartitionSpec as P

adapter_scale = 2.0


def merge_weight_block(resident_matrix, rank_cols, rank_rows):
    adapter_update = lax.dot_general(
        rank_cols, rank_rows, (((0,), (1,)), ((), ())), preferred_element_type=jnp.float32
    )
    return (resident_matrix.astype(jnp.float32) + adapter_scale * adapter_update).astype(
        jnp.bfloat16
    )


def per_device(
    normed,
    resident_gate_matrix,
    resident_up_matrix,
    resident_down_matrix,
    gate_input_factor,
    up_input_factor,
    gate_output_factor,
    up_output_factor,
    down_input_factor,
    down_output_factor,
):
    cols_gate, cols_up, rows_down = (
        lax.all_gather(gate_input_factor, "tp", axis=1, tiled=True),
        lax.all_gather(up_input_factor, "tp", axis=1, tiled=True),
        lax.all_gather(down_output_factor, "tp", axis=0, tiled=True),
    )
    rows_gate, rows_up, cols_down = (
        lax.all_gather(gate_output_factor, "fsdp", axis=0, tiled=True),
        lax.all_gather(up_output_factor, "fsdp", axis=0, tiled=True),
        lax.all_gather(down_input_factor, "fsdp", axis=1, tiled=True),
    )
    refreshed_gate_matrix = merge_weight_block(resident_gate_matrix, cols_gate, rows_gate)
    refreshed_up_matrix = merge_weight_block(resident_up_matrix, cols_up, rows_up)
    refreshed_down_matrix = merge_weight_block(resident_down_matrix, cols_down, rows_down)
    out_rows = normed.shape[1] // lax.axis_size("tp")
    outputs = []
    for number in range(normed.shape[0]):
        states = normed[number]
        gate_part = jnp.dot(states, refreshed_gate_matrix, preferred_element_type=jnp.float32)
        up_part = jnp.dot(states, refreshed_up_matrix, preferred_element_type=jnp.float32)
        gate_sum, up_sum = lax.psum((gate_part, up_part), "fsdp")
        hidden = (jax.nn.silu(gate_sum) * up_sum).astype(jnp.bfloat16)

        def down_term(first_row, row_count, hidden=hidden):
            return jnp.dot(hidden, refreshed_down_matrix, preferred_element_type=jnp.float32)

        summed = lax.psum_scatter(
            down_term(jnp.int32(0), out_rows * lax.axis_size("tp")),
            "tp",
            scatter_dimension=0,
            tiled=True,
        )
        outputs.append(summed.astype(jnp.bfloat16))
    return jnp.stack(outputs, 0)


def solution(mesh):
    in_specs = (
        P(None, None, "fsdp"),
        P("fsdp", "tp"),
        P("fsdp", "tp"),
        P("tp", "fsdp"),
        P(None, ("fsdp", "tp")),
        P(None, ("fsdp", "tp")),
        P(("tp", "fsdp"), None),
        P(("tp", "fsdp"), None),
        P(None, ("tp", "fsdp")),
        P(("fsdp", "tp"), None),
    )
    out_specs = P(None, "tp", "fsdp")
    return jax.shard_map(
        per_device, mesh=mesh, in_specs=in_specs, out_specs=out_specs, check_vma=False
    )
```

profile of v0, /device:TPU:0, one launch (start us, length us, event | category | flops | bytes accessed | tf_op | source)
XLA Modules:
  0.0 401.9 jit_solution(14145466291049470295)
XLA Ops:
  6.5 0.0 all-reduce.3.cloned.1.call-start
  6.5 26.2 %all-gather.1 = bf16[16,208,16]{1,2,0:T(8,128)(2,1)S(1)} all-gather(bf16[1,208,16]{1,2,0:T(8,128)(2,1)} %bitcast.45), channel_id=1, replica_groups=mesh['fsdp'=16,'tp'=8] {'fsdp'}, dimensions={0}, use_global_device_ids=true | all-gather | bytes 113152 | tf_op jit(solution)/shard_map/all_gather | solution.py:37
  32.8 0.2 reshape.3
  33.0 24.2 %all_gather.20 = bf16[16,1024]{1,0:T(8,128)(2,1)S(1)} all-gather(bf16[16,128]{1,0:T(8,128)(2,1)} %param.15), channel_id=1, replica_groups=mesh['fsdp'=16,'tp'=8] {'tp'}, dimensions={1}, use_global_device_ids=true | all-gather | bytes 36864 | tf_op jit(solution)/shard_map/all_gather | solution.py:32
  57.3 0.0 copy-start.5
  57.3 5.0 %add_convert_fusion.1 = bf16[1024,3328]{1,0:T(8,128)(2,1)S(1)} fusion(bf16[1024,3328]{1,0:T(8,128)(2,1)} %param.12, bf16[16,1024]{1,0:T(8,128)(2,1)S(1)} %all_gather.20, bf16[3328,16]{0,1:T(8,128)(2,1)S(1)} %reshape.3), kind=kOutput, calls=%fused_computation.1 | convolution fusion | flops 122683392 | bytes 13770752 | tf_op jit(solution)/shard_map/dot_general | solution.py:10
  62.3 0.0 copy-done.5
  62.3 3.8 convolution_bitcast_fusion
  66.1 0.0 copy-start
  66.1 0.0 copy-start.2
  66.1 3.9 convolution_bitcast_fusion.2
  70.1 0.0 copy-done
  70.1 19.3 %all-gather = bf16[16,208,16]{1,2,0:T(8,128)(2,1)S(1)} all-gather(bf16[1,208,16]{1,2,0:T(8,128)(2,1)S(1)} %bitcast.46), channel_id=1, replica_groups=mesh['fsdp'=16,'tp'=8] {'fsdp'}, dimensions={0}, use_global_device_ids=true | all-gather | bytes 113152 | tf_op jit(solution)/shard_map/all_gather | solution.py:36
  89.4 0.2 reshape.1
  89.6 0.0 copy-done.2
  89.6 23.8 %all_gather.18 = bf16[16,1024]{1,0:T(8,128)(2,1)S(1)} all-gather(bf16[16,128]{1,0:T(8,128)(2,1)S(1)} %copy-done.2), channel_id=1, replica_groups=mesh['fsdp'=16,'tp'=8] {'tp'}, dimensions={1}, use_global_device_ids=true | all-gather | bytes 36864 | tf_op jit(solution)/shard_map/all_gather | solution.py:31
  113.5 4.9 %add_convert_fusion.2 = bf16[1024,3328]{1,0:T(8,128)(2,1)S(1)} fusion(bf16[1024,3328]{1,0:T(8,128)(2,1)} %param.11, bf16[16,1024]{1,0:T(8,128)(2,1)S(1)} %all_gather.18, bf16[3328,16]{0,1:T(8,128)(2,1)S(1)} %reshape.1), kind=kOutput, calls=%fused_computation.2 | convolution fusion | flops 122683392 | bytes 13770752 | tf_op jit(solution)/shard_map/dot_general | solution.py:10
  118.4 3.9 convolution_bitcast_fusion.1
  122.2 3.8 convolution_bitcast_fusion.3
  126.0 0.0 copy-start.1
  126.0 0.0 copy-start.3
  126.0 0.0 all-reduce.3.cloned.1.call-update
  126.1 0.0 reduce-scatter.3.cloned.1.call-start
  126.1 0.6 copy-done.1
  126.7 21.2 %all-gather.2 = bf16[16,208,16]{1,2,0:T(8,128)(2,1)S(1)} all-gather(bf16[1,208,16]{1,2,0:T(8,128)(2,1)S(1)} %bitcast.47), channel_id=1, replica_groups=mesh['fsdp'=16,'tp'=8] {'fsdp'}, dimensions={0}, use_global_device_ids=true | all-gather | bytes 113152 | tf_op jit(solution)/shard_map/all_gather | solution.py:38
  148.0 0.2 reshape.5
  148.2 0.0 copy-done.3
  148.2 23.7 %all_gather.23 = bf16[1024,16]{0,1:T(8,128)(2,1)S(1)} all-gather(bf16[128,16]{0,1:T(8,128)(2,1)S(1)} %copy-done.3), channel_id=1, replica_groups=mesh['fsdp'=16,'tp'=8] {'tp'}, dimensions={0}, use_global_device_ids=true | all-gather | bytes 36864 | tf_op jit(solution)/shard_map/all_gather | solution.py:33
  172.0 7.8 %add_convert_fusion = bf16[3328,1024]{1,0:T(8,128)(2,1)} fusion(bf16[3328,1024]{1,0:T(8,128)(2,1)} %param.13, bf16[3328,16]{0,1:T(8,128)(2,1)S(1)} %reshape.5, bf16[1024,16]{0,1:T(8,128)(2,1)S(1)} %all_gather.23), kind=kOutput, calls=%fused_computation | convolution fusion | flops 122683392 | bytes 13770752 | tf_op jit(solution)/shard_map/dot_general | solution.py:10
  179.8 126.3 %all-reduce.3.cloned.1.call-done = (f32[256,3328]{0,1:T(8,128)}, f32[256,3328]{0,1:T(8,128)}, f32[256,3328]{0,1:T(8,128)}, f32[256,3328]{0,1:T(8,128)}) async-done(((f32[256,3328]{0,1:T(8,128)}, f32[256,3328]{0,1:T(8,128)}, f32[256,3328]{0,1:T(8,128)}, f32[256,3328]{0,1:T(8,128)}), (f32[256,3328]{0,1:T(8,128)}, f32[256,3328]{0,1:T(8,128)}, f32[256,3328]{0,1:T(8,128)}, ...) | async-done | bytes 13631504 | tf_op jit(solution)/shard_map/psum | solution.py:49
  306.1 0.0 copy-start.4
  306.1 8.1 %fusion = f32[256,1024]{1,0:T(8,128)} fusion(bf16[3328,1024]{1,0:T(8,128)(2,1)} %add_convert_fusion, f32[256,3328]{0,1:T(8,128)} %get-tuple-element.7, f32[256,3328]{0,1:T(8,128)} %get-tuple-element.8), kind=kOutput, calls=%fused_computation.9 | convolution fusion | flops 1749942272 | bytes 14680064 | tf_op jit(solution)/shard_map/dot_general | solution.py:53
  314.2 0.0 reduce-scatter.3.cloned.1.call-update
  314.2 0.0 reduce-scatter.5.cloned.1.call-start
  314.3 0.0 copy-done.4
  314.3 6.9 %fusion.1 = f32[256,1024]{1,0:T(8,128)} fusion(bf16[3328,1024]{1,0:T(8,128)(2,1)} %add_convert_fusion, f32[256,3328]{0,1:T(8,128)S(1)} %copy-done.4, f32[256,3328]{0,1:T(8,128)} %get-tuple-element.6), kind=kOutput, calls=%fused_computation.10 | convolution fusion | flops 1749942272 | bytes 14680064 | tf_op jit(solution)/shard_map/dot_general | solution.py:53
  321.2 0.0 reduce-scatter.5.cloned.1.call-update
  321.2 31.8 %reduce-scatter.3.cloned.1.call-done = f32[32,1024]{1,0:T(8,128)} async-done(((f32[256,1024]{1,0:T(8,128)}), f32[32,1024]{1,0:T(8,128)}) %reduce-scatter.3.cloned.1.call-update) | async-done | bytes 131088 | tf_op jit(solution)/shard_map/reduce_scatter | solution.py:55
  353.1 0.9 convert_bitcast_fusion.1
  354.0 39.8 %reduce-scatter.5.cloned.1.call-done = f32[32,1024]{1,0:T(8,128)} async-done(((f32[256,1024]{1,0:T(8,128)}), f32[32,1024]{1,0:T(8,128)}) %reduce-scatter.5.cloned.1.call-update) | async-done | bytes 131088 | tf_op jit(solution)/shard_map/reduce_scatter | solution.py:55
  393.8 0.9 convert_bitcast_fusion
  394.7 0.7 pad_maximum_fusion
  (3 shorter events, 0.1 us)
Async XLA Ops:
  6.5 299.6 %all-reduce.3.cloned.1.call-start = ((), (), s32[]{:S(2)}) async-start(), calls=%async_computation.4 | async-start | bytes 27262976 | tf_op jit(solution)/shard_map/psum | solution.py:49
  57.3 5.0 %copy-start.5 = (bf16[2,256,1024]{2,1,0:T(8,128)(2,1)S(1)}, bf16[2,256,1024]{2,1,0:T(8,128)(2,1)}, u32[]{:S(2)}) copy-start(bf16[2,256,1024]{2,1,0:T(8,128)(2,1)} %param.10) | copy-start | bytes 3145732
  66.1 3.9 copy-start
  66.1 23.5 %copy-start.2 = (bf16[16,128]{1,0:T(8,128)(2,1)S(1)}, bf16[16,128]{1,0:T(8,128)(2,1)}, u32[]{:S(2)}) copy-start(bf16[16,128]{1,0:T(8,128)(2,1)} %param.14) | copy-start | bytes 12292
  126.0 0.7 copy-start.1
  126.0 22.2 %copy-start.3 = (bf16[128,16]{0,1:T(8,128)(2,1)S(1)}, bf16[128,16]{0,1:T(8,128)(2,1)}, u32[]{:S(2)}) copy-start(bf16[128,16]{0,1:T(8,128)(2,1)} %param.19) | copy-start | bytes 12292
  126.1 227.0 %reduce-scatter.3.cloned.1.call-start = ((), (), s32[]{:S(2)}) async-start(), calls=%async_computation.2 | async-start | bytes 1179648 | tf_op jit(solution)/shard_map/reduce_scatter | solution.py:55
  306.1 8.2 %copy-start.4 = (f32[256,3328]{0,1:T(8,128)S(1)}, f32[256,3328]{0,1:T(8,128)}, u32[]{:S(2)}) copy-start(f32[256,3328]{0,1:T(8,128)} %get-tuple-element.5) | copy-start | bytes 10223620
  314.2 79.6 %reduce-scatter.5.cloned.1.call-start = ((), (), s32[]{:S(2)}) async-start(), calls=%async_computation.3 | async-start | bytes 1179648 | tf_op jit(solution)/shard_map/reduce_scatter | solution.py:55
Sparse Core Ops, SparseCore 0:
  126.2 179.8 all-reduce.2
  314.3 38.6 reduce-scatter.2
  355.4 38.3 reduce-scatter.4
where the time goes:
time: 402 us
  waiting for transfers between devices  198 us (49%)
  blocking collectives  139 us (35%)
  matrix products  48.1 us (12%)
  between operations  13.2 us (3%)
    psum x1, waiting for transfers between devices, per_device(): gate_sum, up_sum = lax.psum((gate_part, up_part), 'fsdp')  126 us
    reduce_scatter x2, waiting for transfers between devices, per_device(): lax.psum_scatter(down_term(jnp.int32(0), out_rows * lax.axis_size('tp')),...  71.7 us
    all_gather x1, blocking collectives, per_device(): lax.all_gather(up_output_factor, 'fsdp', axis=0, tiled=True)  26.2 us
    all_gather x1, blocking collectives, per_device(): lax.all_gather(up_input_factor, 'tp', axis=1, tiled=True)  24.2 us
    all_gather x1, blocking collectives, per_device(): lax.all_gather(gate_input_factor, 'tp', axis=1, tiled=True)  23.8 us
    all_gather x1, blocking collectives, per_device(): lax.all_gather(down_output_factor, 'tp', axis=0, tiled=True)  23.7 us
    all_gather x1, blocking collectives, per_device(): lax.all_gather(down_input_factor, 'fsdp', axis=1, tiled=True)  21.2 us
    all_gather x1, blocking collectives, per_device(): lax.all_gather(gate_output_factor, 'fsdp', axis=0, tiled=True)  19.3 us
  transfers between devices with their start and end apart: 3, of which 3 were waited for; matrix products, arithmetic and copies ran while one was open for 4% of the time, Pallas kernels for 0%

commit v1 on v0

v1 whole, which is shorter than its diff:
```python
import functools

import jax
import jax.numpy as jnp
from jax import lax
from jax.experimental import pallas as pl
from jax.experimental.pallas import tpu as pltpu
from jax.sharding import Mesh
from jax.sharding import PartitionSpec as P

adapter_scale = 2.0
f32 = jnp.float32
bf16 = jnp.bfloat16
FSDP = ("yh", "z", "c")
TP = ("x", "yl")
RANK = 16
VMEM_LIMIT = 16 * 1024 * 1024


def pair_bits(core):
    return 1 + 2 * core, 3 - 2 * core


def owner(r, y_first):
    yh, z, c = lax.axis_index("yh"), lax.axis_index("z"), lax.axis_index("c")
    core, bits = (r >> 3) & 1, ((r >> 2) & 1, (r >> 1) & 1, r & 1)
    y, first_z, second_z = bits if y_first else (bits[2], bits[0], bits[1])
    cc = c ^ core
    a, b = pair_bits(cc)
    zz = z ^ (first_z * a) ^ (second_z * b)
    return ((yh ^ y) * 4 + zz) * 2 + cc


def swap(axis, value):
    return lax.ppermute(value, axis, [(0, 1), (1, 0)])


def ring_pair(axis, first, value):
    axes = ("z", "c") if axis == "z" else ("c", "x")

    def index(place, core):
        return place * 2 + core if axis == "z" else core * 4 + place

    moves = []
    for place in range(4):
        for core in range(2):
            step = pair_bits(core)[0 if first else 1]
            moves.append((index(place, core), index(place ^ step, core)))
    return lax.ppermute(value, axes, moves)


def xor_pair(axis, step, value):
    return lax.ppermute(value, axis, [(i, i ^ step) for i in range(4)])


def exchange(axes, value):
    return lax.all_to_all(value, axes, split_axis=0, concat_axis=0)


def in_vmem(body, name, out_shape, *args, behind=(), token=False):
    whole = pl.BlockSpec(memory_space=pltpu.VMEM)
    if token:
        out_shape = (*out_shape, ((8, 128), f32))
    outs = tuple(jax.ShapeDtypeStruct(shape, dtype) for shape, dtype in out_shape)
    moved = sum(a.size * a.dtype.itemsize for a in (*args, *outs))

    def kernel(*refs):
        out_refs = refs[len(args) + len(behind) :]
        if token:
            out_refs[-1][...] = jnp.zeros((8, 128), f32)
            out_refs = out_refs[:-1]
        body(*refs[: len(args)], *out_refs)

    return pl.pallas_call(
        kernel,
        in_specs=[whole] * (len(args) + len(behind)),
        out_specs=[whole] * len(outs),
        out_shape=outs,
        compiler_params=pltpu.CompilerParams(vmem_limit_bytes=VMEM_LIMIT),
        cost_estimate=pl.CostEstimate(flops=moved, bytes_accessed=moved, transcendentals=0),
        name=name,
    )(*args, *behind)


def rows_at(block, size):
    return pl.ds(pl.multiple_of(block * size, 16), size)


def other_core_body(size, y_first, part_ref, send_ref):
    for r in range(8):
        send_ref[r * size : (r + 1) * size] = part_ref[rows_at(owner(8 + r, y_first), size), :]


def core_sum_body(size, y_first, part_ref, recv_ref, keep_ref, send_ref):
    for r in range(8):
        at = r * size
        mine = rows_at(owner(r, y_first), size)
        total = part_ref[mine, :].astype(f32) + recv_ref[at : at + size].astype(f32)
        if r < 4:
            keep_ref[at : at + size] = total
        else:
            send_ref[at - 4 * size : at - 3 * size] = total.astype(bf16)


def halve_body(keep_ref, recv_ref, kept_ref, send_ref):
    half = kept_ref.shape[0]
    kept_ref[...] = keep_ref[:half] + recv_ref[:half].astype(f32)
    send_ref[...] = (keep_ref[half:] + recv_ref[half:].astype(f32)).astype(bf16)


def halve_joined_body(keep_ref, recv_ref, rank_ref, rank_recv_ref, kept_ref, send_ref):
    half = keep_ref.shape[0] // 2
    kept_ref[:half] = keep_ref[:half] + recv_ref[:half].astype(f32)
    send_ref[:half] = (keep_ref[half:] + recv_ref[half:].astype(f32)).astype(bf16)
    rank = rank_ref[...] + rank_recv_ref[...]
    kept_ref[half:] = rank
    send_ref[half:] = rank.astype(bf16)


def halve_tail_body(keep_ref, recv_ref, kept_ref, send_ref):
    half = kept_ref.shape[0] - 2 * RANK
    kept_ref[:half] = keep_ref[:half] + recv_ref[:half].astype(f32)
    send_ref[:half] = (keep_ref[half : 2 * half] + recv_ref[half : 2 * half].astype(f32)).astype(bf16)
    total = keep_ref[2 * half :] + recv_ref[2 * half :].astype(f32)
    kept_ref[half:] = total
    send_ref[half:] = total.astype(bf16)


def halve(body, half, *args):
    shape = (half, args[0].shape[1])
    return in_vmem(body, "halve", [(shape, f32), (shape, bf16)], *args)


def hidden_body(
    gate_ref, gate_recv_ref, up_ref, up_recv_ref, gate_factor_ref, up_factor_ref, down_factor_ref, out_ref
):
    size = gate_factor_ref.shape[1]
    rank = (up_ref[size:] + up_recv_ref[size:].astype(f32)).astype(bf16)
    gate = lax.dot_general(
        gate_factor_ref[...], rank[:RANK], (((0,), (0,)), ((), ())), preferred_element_type=f32
    )
    gate = gate_ref[...] + gate_recv_ref[...].astype(f32) + adapter_scale * gate
    up = lax.dot_general(up_factor_ref[...], rank[RANK:], (((0,), (0,)), ((), ())), preferred_element_type=f32)
    up = up_ref[:size] + up_recv_ref[:size].astype(f32) + adapter_scale * up
    hidden = (gate / (1.0 + jnp.exp(-gate)) * up).astype(bf16)
    low = jnp.dot(down_factor_ref[...], hidden, preferred_element_type=f32).astype(bf16)
    for copy in range(out_ref.shape[0]):
        out_ref[copy, :size] = hidden
        out_ref[copy, size:] = low


def double_body(bit, mine_ref, theirs_ref, out_ref):
    count = mine_ref.shape[0]
    high = bit()
    out_ref[pl.ds(high * count, count)] = mine_ref[...]
    out_ref[pl.ds((1 - high) * count, count)] = theirs_ref[...]


def double_flat_body(bit, mine_ref, theirs_ref, out_ref):
    count, _, width = mine_ref.shape
    high = bit()
    for side, from_ref in ((high, mine_ref), (1 - high, theirs_ref)):
        for i in range(count):
            at = pl.multiple_of((side * count + i) * width, width)
            out_ref[:, pl.ds(at, width)] = from_ref[i]


def add_body(mine_ref, theirs_ref, out_ref):
    out_ref[...] = mine_ref[...] + theirs_ref[...]


def spread_body(mine_ref, theirs_ref, out_ref, low_ref):
    chips, size = mine_ref.shape[0], mine_ref.shape[1] - RANK
    core = lax.axis_index("c")
    low = jnp.zeros(low_ref.shape, f32)
    for chip in range(chips):
        for side, from_ref in enumerate((mine_ref, theirs_ref)):
            out_ref[rows_at(2 * chip + (core if side == 0 else 1 - core), size), :] = from_ref[chip, :size]
            low = low + from_ref[chip, size:].astype(f32)
    low_ref[...] = low.astype(bf16)


def tp_blocks_body(part_ref, low_ref, factor_ref, out_ref):
    blocks, steps, block = out_ref.shape[:3]
    for s in range(steps):
        first = s * blocks * block
        rows = slice(first, first + blocks * block)
        term = lax.dot_general(
            low_ref[:, rows], factor_ref[2 * RANK :], (((0,), (0,)), ((), ())), preferred_element_type=f32
        )
        total = (part_ref[rows] + adapter_scale * term).astype(bf16)
        for t in range(blocks):
            out_ref[t, s] = total[t * block : (t + 1) * block]


def owner_sum_body(blocks_ref, out_ref):
    total = blocks_ref[0].astype(f32)
    for t in range(1, blocks_ref.shape[0]):
        total = total + blocks_ref[t].astype(f32)
    out_ref[...] = total.astype(bf16)


def after(value, earlier):
    return lax.optimization_barrier((value, earlier))[0]


def per_device(
    normed,
    resident_gate_matrix,
    resident_up_matrix,
    resident_down_matrix,
    gate_input_factor,
    up_input_factor,
    gate_output_factor,
    up_output_factor,
    down_input_factor,
    down_output_factor,
):
    steps, rows, depth = normed.shape
    units = resident_gate_matrix.shape[1]
    size = units // 16
    lanes = steps * rows
    states = normed.reshape(lanes, depth)
    near, far, across = (
        functools.partial(ring_pair, "z", True),
        functools.partial(ring_pair, "z", False),
        functools.partial(swap, "yh"),
    )

    wide = jnp.concatenate([gate_input_factor, up_input_factor, down_output_factor.T], 0)[None]
    (wide,) = in_vmem(
        functools.partial(double_body, lambda: lax.axis_index("yl")),
        "double",
        [((2, *wide.shape[1:]), bf16)],
        wide,
        swap("yl", wide),
    )
    parts = [
        lax.dot_general(w, states, (((0,), (1,)), ((), ())), preferred_element_type=f32).astype(bf16)
        for w in (resident_gate_matrix, resident_up_matrix)
    ]
    recvs, sums, tokens = [], [], []
    for part, y_first in zip(parts, (True, False)):
        (send,) = in_vmem(
            functools.partial(other_core_body, size, y_first), "other_core", [((units // 2, lanes), bf16)], part, behind=(wide,)
        )
        recvs.append(swap("c", send))
    for part, recv, y_first in zip(parts, recvs, (True, False)):
        shape = (4 * size, lanes)
        keep, send, token = in_vmem(
            functools.partial(core_sum_body, size, y_first),
            "core_sum",
            [(shape, f32), (shape, bf16)],
            part,
            recv,
            behind=tokens,
            token=True,
        )
        sums.append((keep, send))
        tokens = [token]
    wide = after(wide, token)
    (wide,) = in_vmem(
        functools.partial(double_body, lambda: lax.axis_index("x") & 1),
        "double",
        [((4, *wide.shape[1:]), bf16)],
        wide,
        xor_pair("x", 1, wide),
    )
    (wide,) = in_vmem(
        functools.partial(double_flat_body, lambda: lax.axis_index("x") >> 1),
        "double",
        [((3 * RANK, depth), bf16)],
        wide,
        xor_pair("x", 3, wide),
    )
    rank = lax.dot_general(
        wide[: 2 * RANK], states, (((1,), (1,)), ((), ())), preferred_element_type=f32
    )
    (rank,) = in_vmem(add_body, "add", [(rank.shape, f32)], rank, swap("c", rank))

    keep, send = sums[0]
    keep, send = halve(halve_body, 2 * size, keep, across(send))
    keep, send = halve(halve_body, size, keep, near(send))
    gate = keep, far(send)
    keep, send = sums[1]
    keep, send = halve(halve_joined_body, 2 * size + 2 * RANK, keep, near(send), rank, near(rank))
    keep, send = halve(halve_tail_body, size + 2 * RANK, keep, far(send))
    up = keep, across(send)
    (hidden,) = in_vmem(
        hidden_body,
        "hidden",
        [((8, size + RANK, lanes), bf16)],
        *gate,
        *up,
        gate_output_factor.T,
        up_output_factor.T,
        down_input_factor,
    )
    hidden = exchange(("yh", "z"), hidden)
    hidden, low = in_vmem(
        spread_body, "spread", [((units, lanes), bf16), ((RANK, lanes), bf16)], hidden, swap("c", hidden)
    )
    part = lax.dot_general(
        hidden, resident_down_matrix, (((0,), (0,)), ((), ())), preferred_element_type=f32
    )
    (blocks,) = in_vmem(
        tp_blocks_body,
        "tp_blocks",
        [((8, steps, rows // 8, part.shape[1]), bf16)],
        part,
        low,
        wide,
    )
    blocks = exchange(TP, blocks)
    return in_vmem(owner_sum_body, "owner_sum", [(blocks.shape[1:], bf16)], blocks)[0]


def solution(mesh):
    fine = Mesh(mesh.devices.reshape(2, 4, 2, 4, 2), FSDP + TP)
    fsdp, tp = FSDP, TP
    in_specs = (
        P(None, None, fsdp),
        P(fsdp, tp),
        P(fsdp, tp),
        P(tp, fsdp),
        P(None, fsdp + tp),
        P(None, fsdp + tp),
        P(tp + fsdp, None),
        P(tp + fsdp, None),
        P(None, tp + fsdp),
        P(fsdp + tp, None),
    )
    out_specs = P(None, tp, fsdp)
    return jax.shard_map(
        per_device, mesh=fine, in_specs=in_specs, out_specs=out_specs, check_vma=False
    )
```

time: 402 us -> 117 us (0.29)
  waiting for transfers between devices: 198 us -> 31.9 us
  blocking collectives: 139 us -> 48.1 us
  matrix products: 48.1 us -> 15.4 us
  starting transfers between devices: 0.09 us -> 16.6 us
  between operations: 13.2 us -> 0.21 us
  Pallas kernels: 0 us -> 4.21 us
    all_gather x6 -> x0, blocking collectives: 139 us -> none  [the longest x1 26.2 us: per_device(): lax.all_gather(up_output_factor, 'fsdp', axis=0, tiled=True)]
    psum x1 -> x0, waiting for transfers between devices: 126 us -> none  [per_device(): gate_sum, up_sum = lax.psum((gate_part, up_part), 'fsdp')]
    reduce_scatter x2 -> x0, waiting for transfers between devices: 71.7 us -> none  [per_device(): lax.psum_scatter(down_term(jnp.int32(0), out_rows * lax.axis_size('tp')),...]
    all_to_all x0 -> x2, blocking collectives: none -> 48.1 us  [exchange(): return lax.all_to_all(value, axes, split_axis=0, concat_axis=0)]
    dot_general x9 -> x4, matrix products: 48.1 us -> 15.4 us  [the longest x2 11.3 us: per_device(): lax.dot_general(w, states, (((0,), (1,)), ((), ())), preferred_element_ty...]
    ppermute x0 -> x14, waiting for transfers between devices: none -> 31.9 us  [the longest x5 17.8 us: ring_pair(): return lax.ppermute(value, axes, moves)]
    ppermute x0 -> x14, starting transfers between devices: none -> 16.6 us  [the longest x5 6.84 us: ring_pair(): return lax.ppermute(value, axes, moves)]
    pallas_call x0 -> x16, Pallas kernels: none -> 4.21 us  [in_vmem(): pl.pallas_call(kernel, in_specs=[whole] * (len(args) + len(behind)), out_...]
  transfers between devices with their start and end apart: 3 -> 14, of which waited for: 3 -> 10; matrix products, arithmetic and copies ran while one was open for 4% -> 10% of each run, Pallas kernels for 0% -> 1%
where the time goes in v1:
time: 117 us
  blocking collectives  48.1 us (41%)
  waiting for transfers between devices  31.9 us (27%)
  starting transfers between devices  16.6 us (14%)
  matrix products  15.4 us (13%)
  Pallas kernels  4.21 us (4%)
    all_to_all x2, blocking collectives, exchange(): return lax.all_to_all(value, axes, split_axis=0, concat_axis=0)  48.1 us
    ppermute x5, waiting for transfers between devices, ring_pair(): return lax.ppermute(value, axes, moves)  17.8 us
    dot_general x2, matrix products, per_device(): lax.dot_general(w, states, (((0,), (1,)), ((), ())), preferred_element_ty...  11.3 us
    ppermute x7, waiting for transfers between devices, swap(): return lax.ppermute(value, axis, [(0, 1), (1, 0)])  8.75 us
    ppermute x5, starting transfers between devices, ring_pair(): return lax.ppermute(value, axes, moves)  6.84 us
    ppermute x7, starting transfers between devices, swap(): return lax.ppermute(value, axis, [(0, 1), (1, 0)])  5.52 us
    ppermute x2, waiting for transfers between devices, xor_pair(): return lax.ppermute(value, axis, [(i, i ^ step) for i in range(4)])  5.31 us
    ppermute x2, starting transfers between devices, xor_pair(): return lax.ppermute(value, axis, [(i, i ^ step) for i in range(4)])  4.25 us
  transfers between devices with their start and end apart: 14, of which 10 were waited for; matrix products, arithmetic and copies ran while one was open for 10% of the time, Pallas kernels for 1%

profile of v1, /device:TPU:0, one launch (start us, length us, event | category | flops | bytes accessed | tf_op | source)
XLA Modules:
  0.0 117.2 jit_solution(9445769744995447021)
XLA Ops:
  0.0 0.0 copy-start
  0.0 0.8 maximum_bitcast_fusion.refs_0_
  0.8 1.7 %collective-permute-start = (bf16[1,48,128]{2,1,0:T(8,128)(2,1)S(1)}, bf16[1,48,128]{2,1,0:T(8,128)(2,1)S(1)}, u32[]{:S(2)}, u32[]{:S(2)}) collective-permute-start(bf16[1,48,128]{2,1,0:T(8,128)(2,1)S(1)} %maximum_bitcast_fusion.refs_0_), channel_id=1, source_target_pairs={{0,1},{1,0},{2,3},{3,2},{4,5},{5,4},{6,7},{7,6},{8,9},{9,8},{10,11... | collective-permute-start | bytes 36872 | tf_op jit(solution)/shard_map/ppermute | solution.py:35
  2.5 0.0 copy-done
  2.5 0.0 slice-start
  2.5 0.0 slice-start.1
  2.5 7.1 %convolution_convert_fusion.1.refs_0_ = bf16[3328,512]{1,0:T(8,128)(2,1)S(1)} fusion(bf16[1024,3328]{1,0:T(8,128)(2,1)} %param.11, bf16[512,1024]{1,0:T(8,128)(2,1)S(1)} %bitcast.13), kind=kOutput, calls=%fused_computation.1 | convolution fusion | flops 3491364864 | bytes 11272192 | tf_op jit(solution)/shard_map/dot_general | solution.py:239
  9.6 0.0 collective-permute-done.refs_1_
  9.6 0.1 other_core.2
  9.7 0.1 collective-permute-start.1
  9.8 0.0 slice-done
  9.8 0.0 slice-done.1
  9.9 4.2 %convolution_convert_fusion.refs_0_ = bf16[3328,512]{1,0:T(8,128)(2,1)S(1)} fusion(bf16[1024,3328]{1,0:T(8,128)(2,1)S(1)} %bitcast.20, bf16[512,1024]{1,0:T(8,128)(2,1)S(1)} %bitcast.14), kind=kOutput, calls=%fused_computation | convolution fusion | flops 3491364864 | bytes 11272192 | tf_op jit(solution)/shard_map/dot_general | solution.py:239
  14.1 0.1 other_core.3
  14.2 0.5 collective-permute-start.5
  14.7 0.0 collective-permute-done.1.refs_1_
  14.8 0.4 core_sum.2
  15.1 2.8 %collective-permute-done.5.refs_1_ = bf16[1664,512]{1,0:T(8,128)(2,1)S(1)} collective-permute-done((bf16[1664,512]{1,0:T(8,128)(2,1)S(1)}, bf16[1664,512]{1,0:T(8,128)(2,1)S(1)}, u32[]{:S(2)}, u32[]{:S(2)}) %collective-permute-start.5) | collective-permute-done | bytes 1703968 | tf_op jit(solution)/shard_map/ppermute | solution.py:35
  18.0 0.9 core_sum.3
  18.8 1.9 %collective-permute-start.6 = (bf16[832,512]{1,0:T(8,128)(2,1)S(1)}, bf16[832,512]{1,0:T(8,128)(2,1)S(1)}, u32[]{:S(2)}, u32[]{:S(2)}) collective-permute-start(bf16[832,512]{1,0:T(8,128)(2,1)S(1)} %get-tuple-element.28), channel_id=1, source_target_pairs={{0,16},{8,56},{16,0},{24,40},{32,48},{40,24},{48,32},{56,8},{1,17}... | collective-permute-start | bytes 2555912 | tf_op jit(solution)/shard_map/ppermute | solution.py:49
  20.7 2.9 %collective-permute-start.2 = (bf16[832,512]{1,0:T(8,128)(2,1)S(1)}, bf16[832,512]{1,0:T(8,128)(2,1)S(1)}, u32[]{:S(2)}, u32[]{:S(2)}) collective-permute-start(bf16[832,512]{1,0:T(8,128)(2,1)S(1)} %get-tuple-element.21), channel_id=1, source_target_pairs={{0,64},{64,0},{1,65},{65,1},{2,66},{66,2},{3,67},{67,3},{4,68},{68... | collective-permute-start | bytes 2555912 | tf_op jit(solution)/shard_map/ppermute | solution.py:35
  23.7 1.5 %collective-permute-start.7 = (bf16[2,48,128]{2,1,0:T(8,128)(2,1)S(1)}, bf16[2,48,128]{2,1,0:T(8,128)(2,1)S(1)}, u32[]{:S(2)}, u32[]{:S(2)}) collective-permute-start(bf16[2,48,128]{2,1,0:T(8,128)(2,1)S(1)} %double.3.refs_1_.refs_0_), channel_id=1, source_target_pairs={{0,2},{2,0},{4,6},{6,4},{1,3},{3,1},{5,7},{7,5},{8,10},{10,8},{12,... | collective-permute-start | bytes 73736 | tf_op jit(solution)/shard_map/ppermute | solution.py:53
  25.2 2.3 %collective-permute-done.7.refs_1_ = bf16[2,48,128]{2,1,0:T(8,128)(2,1)S(1)} collective-permute-done((bf16[2,48,128]{2,1,0:T(8,128)(2,1)S(1)}, bf16[2,48,128]{2,1,0:T(8,128)(2,1)S(1)}, u32[]{:S(2)}, u32[]{:S(2)}) %collective-permute-start.7) | collective-permute-done | bytes 24608 | tf_op jit(solution)/shard_map/ppermute | solution.py:53
  27.5 2.7 %collective-permute-start.8 = (bf16[4,48,128]{2,1,0:T(8,128)(2,1)S(1)}, bf16[4,48,128]{2,1,0:T(8,128)(2,1)S(1)}, u32[]{:S(2)}, u32[]{:S(2)}) collective-permute-start(bf16[4,48,128]{2,1,0:T(8,128)(2,1)S(1)} %double.4.refs_0_), channel_id=1, source_target_pairs={{0,6},{2,4},{4,2},{6,0},{1,7},{3,5},{5,3},{7,1},{8,14},{10,12},{12... | collective-permute-start | bytes 147464 | tf_op jit(solution)/shard_map/ppermute | solution.py:53
  30.2 3.0 %collective-permute-done.8.refs_1_ = bf16[4,48,128]{2,1,0:T(8,128)(2,1)S(1)} collective-permute-done((bf16[4,48,128]{2,1,0:T(8,128)(2,1)S(1)}, bf16[4,48,128]{2,1,0:T(8,128)(2,1)S(1)}, u32[]{:S(2)}, u32[]{:S(2)}) %collective-permute-start.8) | collective-permute-done | bytes 49184 | tf_op jit(solution)/shard_map/ppermute | solution.py:53
  33.3 0.4 fusion.refs_0_
  33.7 0.2 collective-permute-start.9
  33.9 1.0 collective-permute-done.9.refs_1_
  35.0 0.1 collective-permute-start.10
  35.1 4.3 %collective-permute-done.10.refs_3_ = f32[32,512]{1,0:T(8,128)S(1)} collective-permute-done((f32[32,512]{1,0:T(8,128)S(1)}, f32[32,512]{1,0:T(8,128)S(1)}, u32[]{:S(2)}, u32[]{:S(2)}) %collective-permute-start.10) | collective-permute-done | bytes 65568 | tf_op jit(solution)/shard_map/ppermute | solution.py:49
  39.3 0.0 collective-permute-done.6.refs_1_
  39.3 0.0 copy-start.1
  39.3 0.0 copy-start.2
  39.3 0.0 copy-start.3
  39.3 0.2 halve.6
  39.5 2.2 %collective-permute-start.11 = (bf16[448,512]{1,0:T(8,128)(2,1)S(1)}, bf16[448,512]{1,0:T(8,128)(2,1)S(1)}, u32[]{:S(2)}, u32[]{:S(2)}) collective-permute-start(bf16[448,512]{1,0:T(8,128)(2,1)S(1)} %get-tuple-element.30), channel_id=1, source_target_pairs={{0,48},{8,24},{16,32},{24,8},{32,16},{40,56},{48,0},{56,40},{1,49}... | collective-permute-start | bytes 1376264 | tf_op jit(solution)/shard_map/ppermute | solution.py:49
  41.7 1.1 collective-permute-done.2.refs_1_
  42.8 0.0 slice-start.2
  42.8 0.2 halve.4
  43.0 0.6 collective-permute-start.3
  43.5 7.0 %collective-permute-done.11.refs_1_ = bf16[448,512]{1,0:T(8,128)(2,1)S(1)} collective-permute-done((bf16[448,512]{1,0:T(8,128)(2,1)S(1)}, bf16[448,512]{1,0:T(8,128)(2,1)S(1)}, u32[]{:S(2)}, u32[]{:S(2)}) %collective-permute-start.11) | collective-permute-done | bytes 458784 | tf_op jit(solution)/shard_map/ppermute | solution.py:49
  50.6 0.1 halve.7
  50.7 0.1 collective-permute-start.12
  50.7 1.5 %collective-permute-done.3.refs_1_ = bf16[416,512]{1,0:T(8,128)(2,1)S(1)} collective-permute-done((bf16[416,512]{1,0:T(8,128)(2,1)S(1)}, bf16[416,512]{1,0:T(8,128)(2,1)S(1)}, u32[]{:S(2)}, u32[]{:S(2)}) %collective-permute-start.3) | collective-permute-done | bytes 426016 | tf_op jit(solution)/shard_map/ppermute | solution.py:49
  52.3 0.1 halve.5
  52.4 2.1 %collective-permute-start.4 = (bf16[208,512]{1,0:T(8,128)(2,1)S(1)}, bf16[208,512]{1,0:T(8,128)(2,1)S(1)}, u32[]{:S(2)}, u32[]{:S(2)}) collective-permute-start(bf16[208,512]{1,0:T(8,128)(2,1)S(1)} %get-tuple-element.25), channel_id=1, source_target_pairs={{0,48},{8,24},{16,32},{24,8},{32,16},{40,56},{48,0},{56,40},{1,49}... | collective-permute-start | bytes 638984 | tf_op jit(solution)/shard_map/ppermute | solution.py:49
  54.5 5.0 %collective-permute-done.4.refs_1_ = bf16[208,512]{1,0:T(8,128)(2,1)S(1)} collective-permute-done((bf16[208,512]{1,0:T(8,128)(2,1)S(1)}, bf16[208,512]{1,0:T(8,128)(2,1)S(1)}, u32[]{:S(2)}, u32[]{:S(2)}) %collective-permute-start.4) | collective-permute-done | bytes 213024 | tf_op jit(solution)/shard_map/ppermute | solution.py:49
  59.5 0.0 collective-permute-done.12.refs_3_
  59.5 0.0 copy-done.1
  59.5 0.0 copy-done.2
  59.5 0.0 copy-done.3
  59.5 0.0 slice-start.3
  59.5 0.6 hidden.1
  60.1 28.6 %all_to_all.10.refs_0_ = bf16[8,224,512]{2,1,0:T(8,128)(2,1)S(1)} all-to-all(bf16[8,224,512]{2,1,0:T(8,128)(2,1)S(1)} %hidden.1), channel_id=1, replica_groups=mesh['yh'=2,'z'=4,'c'=2,'x'=4,'yl'=2] {'yh','z'}, dimensions={0} | all-to-all | bytes 3670016 | tf_op jit(solution)/shard_map/all_to_all | solution.py:57
  88.7 0.0 collective-permute-start.13
  88.7 3.8 %collective-permute-done.13.refs_1_ = bf16[8,224,512]{2,1,0:T(8,128)(2,1)S(1)} collective-permute-done((bf16[8,224,512]{2,1,0:T(8,128)(2,1)S(1)}, bf16[8,224,512]{2,1,0:T(8,128)(2,1)S(1)}, u32[]{:S(2)}, u32[]{:S(2)}) %collective-permute-start.13) | collective-permute-done | bytes 1835040 | tf_op jit(solution)/shard_map/ppermute | solution.py:35
  92.5 0.3 spread.1
  92.8 0.0 slice-done.2
  92.8 0.0 slice-done.3
  92.8 3.7 %fusion.2.refs_0_ = f32[512,1024]{1,0:T(8,128)S(1)} fusion(bf16[3328,512]{1,0:T(8,128)(2,1)S(1)} %get-tuple-element.33, bf16[3328,1024]{1,0:T(8,128)(2,1)S(1)} %bitcast.22), kind=kOutput, calls=%fused_computation.5 | convolution fusion | flops 3489660928 | bytes 12320768 | tf_op jit(solution)/shard_map/dot_general | solution.py:303
  96.5 0.5 tp_blocks.1
  97.0 19.5 %all_to_all.11.refs_0_ = bf16[8,2,32,1024]{3,2,1,0:T(8,128)(2,1)S(1)} all-to-all(bf16[8,2,32,1024]{3,2,1,0:T(8,128)(2,1)S(1)} %tp_blocks.1), channel_id=1, replica_groups=mesh['yh'=2,'z'=4,'c'=2,'x'=4,'yl'=2] {'x','yl'}, dimensions={0} | all-to-all | bytes 2097152 | tf_op jit(solution)/shard_map/all_to_all | solution.py:57
  116.4 0.8 owner_sum.1
  (6 shorter events, 0.1 us)
Async XLA Ops:
  0.0 2.5 %copy-start = (bf16[2,256,1024]{2,1,0:T(8,128)(2,1)S(1)}, bf16[2,256,1024]{2,1,0:T(8,128)(2,1)}, u32[]{:S(2)}) copy-start(bf16[2,256,1024]{2,1,0:T(8,128)(2,1)} %param.10) | copy-start | bytes 3145732
  0.8 8.8 %collective-permute-start = (bf16[1,48,128]{2,1,0:T(8,128)(2,1)S(1)}, bf16[1,48,128]{2,1,0:T(8,128)(2,1)S(1)}, u32[]{:S(2)}, u32[]{:S(2)}) collective-permute-start(bf16[1,48,128]{2,1,0:T(8,128)(2,1)S(1)} %maximum_bitcast_fusion.refs_0_), channel_id=1, source_target_pairs={{0,1},{1,0},{2,3},{3,2},{4,5},{5,4},{6,7},{7,6},{8,9},{9,8},{10,11... | collective-permute-start | bytes 36872 | tf_op jit(solution)/shard_map/ppermute | solution.py:35
  2.5 7.4 %slice-start = ((s8[6815744]{0:T(1024)(128)(4,1)}), s8[4194304]{0:T(1024)(128)(4,1)S(1)}, s32[]{:S(2)}) async-start(s8[6815744]{0:T(1024)(128)(4,1)} %bitcast.19), calls=%async_computation.2 | async-start | bytes 8388608
  2.5 7.4 %slice-start.1 = ((s8[6815744]{0:T(1024)(128)(4,1)}), s8[2621440]{0:T(1024)(128)(4,1)S(1)}, s32[]{:S(2)}) async-start(s8[6815744]{0:T(1024)(128)(4,1)} %bitcast.19), calls=%async_computation.3 | async-start | bytes 5242880
  9.7 5.0 %collective-permute-start.1 = (bf16[1664,512]{1,0:T(8,128)(2,1)S(1)}, bf16[1664,512]{1,0:T(8,128)(2,1)S(1)}, u32[]{:S(2)}, u32[]{:S(2)}) collective-permute-start(bf16[1664,512]{1,0:T(8,128)(2,1)S(1)} %other_core.2), channel_id=1, source_target_pairs={{0,8},{8,0},{1,9},{9,1},{2,10},{10,2},{3,11},{11,3},{4,12},{12,4},... | collective-permute-start | bytes 5111816 | tf_op jit(solution)/shard_map/ppermute | solution.py:35
  14.2 3.8 %collective-permute-start.5 = (bf16[1664,512]{1,0:T(8,128)(2,1)S(1)}, bf16[1664,512]{1,0:T(8,128)(2,1)S(1)}, u32[]{:S(2)}, u32[]{:S(2)}) collective-permute-start(bf16[1664,512]{1,0:T(8,128)(2,1)S(1)} %other_core.3), channel_id=1, source_target_pairs={{0,8},{8,0},{1,9},{9,1},{2,10},{10,2},{3,11},{11,3},{4,12},{12,4},... | collective-permute-start | bytes 5111816 | tf_op jit(solution)/shard_map/ppermute | solution.py:35
  18.8 20.5 %collective-permute-start.6 = (bf16[832,512]{1,0:T(8,128)(2,1)S(1)}, bf16[832,512]{1,0:T(8,128)(2,1)S(1)}, u32[]{:S(2)}, u32[]{:S(2)}) collective-permute-start(bf16[832,512]{1,0:T(8,128)(2,1)S(1)} %get-tuple-element.28), channel_id=1, source_target_pairs={{0,16},{8,56},{16,0},{24,40},{32,48},{40,24},{48,32},{56,8},{1,17}... | collective-permute-start | bytes 2555912 | tf_op jit(solution)/shard_map/ppermute | solution.py:49
  20.7 22.0 %collective-permute-start.2 = (bf16[832,512]{1,0:T(8,128)(2,1)S(1)}, bf16[832,512]{1,0:T(8,128)(2,1)S(1)}, u32[]{:S(2)}, u32[]{:S(2)}) collective-permute-start(bf16[832,512]{1,0:T(8,128)(2,1)S(1)} %get-tuple-element.21), channel_id=1, source_target_pairs={{0,64},{64,0},{1,65},{65,1},{2,66},{66,2},{3,67},{67,3},{4,68},{68... | collective-permute-start | bytes 2555912 | tf_op jit(solution)/shard_map/ppermute | solution.py:35
  23.7 3.8 %collective-permute-start.7 = (bf16[2,48,128]{2,1,0:T(8,128)(2,1)S(1)}, bf16[2,48,128]{2,1,0:T(8,128)(2,1)S(1)}, u32[]{:S(2)}, u32[]{:S(2)}) collective-permute-start(bf16[2,48,128]{2,1,0:T(8,128)(2,1)S(1)} %double.3.refs_1_.refs_0_), channel_id=1, source_target_pairs={{0,2},{2,0},{4,6},{6,4},{1,3},{3,1},{5,7},{7,5},{8,10},{10,8},{12,... | collective-permute-start | bytes 73736 | tf_op jit(solution)/shard_map/ppermute | solution.py:53
  27.5 5.7 %collective-permute-start.8 = (bf16[4,48,128]{2,1,0:T(8,128)(2,1)S(1)}, bf16[4,48,128]{2,1,0:T(8,128)(2,1)S(1)}, u32[]{:S(2)}, u32[]{:S(2)}) collective-permute-start(bf16[4,48,128]{2,1,0:T(8,128)(2,1)S(1)} %double.4.refs_0_), channel_id=1, source_target_pairs={{0,6},{2,4},{4,2},{6,0},{1,7},{3,5},{5,3},{7,1},{8,14},{10,12},{12... | collective-permute-start | bytes 147464 | tf_op jit(solution)/shard_map/ppermute | solution.py:53
  33.7 1.3 %collective-permute-start.9 = (f32[32,512]{1,0:T(8,128)S(1)}, f32[32,512]{1,0:T(8,128)S(1)}, u32[]{:S(2)}, u32[]{:S(2)}) collective-permute-start(f32[32,512]{1,0:T(8,128)S(1)} %fusion.refs_0_), channel_id=1, source_target_pairs={{0,8},{8,0},{1,9},{9,1},{2,10},{10,2},{3,11},{11,3},{4,12},{12,4},... | collective-permute-start | bytes 196616 | tf_op jit(solution)/shard_map/ppermute | solution.py:35
  35.0 4.3 %collective-permute-start.10 = (f32[32,512]{1,0:T(8,128)S(1)}, f32[32,512]{1,0:T(8,128)S(1)}, u32[]{:S(2)}, u32[]{:S(2)}) collective-permute-start(f32[32,512]{1,0:T(8,128)S(1)} %add.1.refs_2_), channel_id=1, source_target_pairs={{0,16},{8,56},{16,0},{24,40},{32,48},{40,24},{48,32},{56,8},{1,17}... | collective-permute-start | bytes 196616 | tf_op jit(solution)/shard_map/ppermute | solution.py:49
  39.3 20.2 %copy-start.1 = (bf16[208,16]{0,1:T(8,128)(2,1)S(1)}, bf16[208,16]{0,1:T(8,128)(2,1)}, u32[]{:S(2)}) copy-start(bf16[208,16]{0,1:T(8,128)(2,1)} %param.16) | copy-start | bytes 19972
  39.3 20.2 %copy-start.2 = (bf16[208,16]{0,1:T(8,128)(2,1)S(1)}, bf16[208,16]{0,1:T(8,128)(2,1)}, u32[]{:S(2)}) copy-start(bf16[208,16]{0,1:T(8,128)(2,1)} %param.17) | copy-start | bytes 19972
  39.3 20.2 %copy-start.3 = (bf16[16,208]{1,0:T(8,128)(2,1)S(1)}, bf16[16,208]{1,0:T(8,128)(2,1)}, u32[]{:S(2)}) copy-start(bf16[16,208]{1,0:T(8,128)(2,1)} %refs_6_.1) | copy-start | bytes 19972
  39.5 11.0 %collective-permute-start.11 = (bf16[448,512]{1,0:T(8,128)(2,1)S(1)}, bf16[448,512]{1,0:T(8,128)(2,1)S(1)}, u32[]{:S(2)}, u32[]{:S(2)}) collective-permute-start(bf16[448,512]{1,0:T(8,128)(2,1)S(1)} %get-tuple-element.30), channel_id=1, source_target_pairs={{0,48},{8,24},{16,32},{24,8},{32,16},{40,56},{48,0},{56,40},{1,49}... | collective-permute-start | bytes 1376264 | tf_op jit(solution)/shard_map/ppermute | solution.py:49
  42.8 50.0 %slice-start.2 = ((s8[6815744]{0:T(1024)(128)(4,1)}), s8[4194304]{0:T(1024)(128)(4,1)S(1)}, s32[]{:S(2)}) async-start(s8[6815744]{0:T(1024)(128)(4,1)} %bitcast.21), calls=%async_computation.4 | async-start | bytes 8388608
  43.0 9.3 %collective-permute-start.3 = (bf16[416,512]{1,0:T(8,128)(2,1)S(1)}, bf16[416,512]{1,0:T(8,128)(2,1)S(1)}, u32[]{:S(2)}, u32[]{:S(2)}) collective-permute-start(bf16[416,512]{1,0:T(8,128)(2,1)S(1)} %get-tuple-element.23), channel_id=1, source_target_pairs={{0,16},{8,56},{16,0},{24,40},{32,48},{40,24},{48,32},{56,8},{1,17}... | collective-permute-start | bytes 1277960 | tf_op jit(solution)/shard_map/ppermute | solution.py:49
  50.7 8.8 %collective-permute-start.12 = (bf16[240,512]{1,0:T(8,128)(2,1)S(1)}, bf16[240,512]{1,0:T(8,128)(2,1)S(1)}, u32[]{:S(2)}, u32[]{:S(2)}) collective-permute-start(bf16[240,512]{1,0:T(8,128)(2,1)S(1)} %get-tuple-element.32), channel_id=1, source_target_pairs={{0,64},{64,0},{1,65},{65,1},{2,66},{66,2},{3,67},{67,3},{4,68},{68... | collective-permute-start | bytes 737288 | tf_op jit(solution)/shard_map/ppermute | solution.py:35
  52.4 7.1 %collective-permute-start.4 = (bf16[208,512]{1,0:T(8,128)(2,1)S(1)}, bf16[208,512]{1,0:T(8,128)(2,1)S(1)}, u32[]{:S(2)}, u32[]{:S(2)}) collective-permute-start(bf16[208,512]{1,0:T(8,128)(2,1)S(1)} %get-tuple-element.25), channel_id=1, source_target_pairs={{0,48},{8,24},{16,32},{24,8},{32,16},{40,56},{48,0},{56,40},{1,49}... | collective-permute-start | bytes 638984 | tf_op jit(solution)/shard_map/ppermute | solution.py:49
  59.5 33.3 %slice-start.3 = ((s8[6815744]{0:T(1024)(128)(4,1)}), s8[2621440]{0:T(1024)(128)(4,1)S(1)}, s32[]{:S(2)}) async-start(s8[6815744]{0:T(1024)(128)(4,1)} %bitcast.21), calls=%async_computation.5 | async-start | bytes 5242880
  88.7 3.8 %collective-permute-start.13 = (bf16[8,224,512]{2,1,0:T(8,128)(2,1)S(1)}, bf16[8,224,512]{2,1,0:T(8,128)(2,1)S(1)}, u32[]{:S(2)}, u32[]{:S(2)}) collective-permute-start(bf16[8,224,512]{2,1,0:T(8,128)(2,1)S(1)} %all_to_all.10.refs_0_), channel_id=1, source_target_pairs={{0,8},{8,0},{1,9},{9,1},{2,10},{10,2},{3,11},{11,3},{4,12},{12,4},... | collective-permute-start | bytes 5505032 | tf_op jit(solution)/shard_map/ppermute | solution.py:35
